TPU v7x, 256 devices: a whole 4x4x8 slice. The times are simulated.
256 devices in a mesh: seq: 32 (over y, x, core), head: 8 (over z).
Axes of the slice: x: 4, y: 4, z: 8, core: 2. Of those that a mesh axis runs over, the one named last changes fastest.
Arguments:
- queries: bfloat16 [32, 128, 16384], P('seq', None, 'head'), parts along dimension 2
- cache_keys: bfloat16 [262144, 1024], P('seq', 'head'), parts along dimension 1
- cache_values: bfloat16 [262144, 1024], P('seq', 'head'), parts along dimension 1
- lengths: int32 [32], replicated, may hold values from 1 to 8192, as said below
- span_owner: int32 [1], replicated, may hold values from 0 to 31
Outputs:
- attended: bfloat16 [32, 128, 16384], P('seq', None, 'head'), parts along dimension 2
There are 8 independent parts, one for each index of `head`. A program takes and returns all parts, laid end to end along the dimension named above; an argument that names none is the same for every part. Nothing has to cross between parts.
Inputs may be any that keep to these rules, and one draw needn't show every extreme that they name: `lengths`: every shard but the last holds 8192 valid positions.
All inputs are finite; a program needn't handle non-finite values.
Results may differ from a plain program's by a relative error of at most 0.0019.
Values may be sent and summed in bfloat16 or wider, within the bound.
No kernel may reach another device: no remote copies, remote signals or barrier semaphores. Data moves between devices by JAX's collectives and lax.ppermute only.
A program may use at most 128 MiB of HBM per device.

v0:
```python
import jax
import jax.numpy as jnp
from jax import lax
from jax.sharding import PartitionSpec as P


def spread(array, axis, root):
    mine = lax.axis_index(axis) == root
    return lax.psum(jnp.where(mine, array, jnp.zeros_like(array)), axis)


def combined_all(part, axis, combine):
    gathered = jax.tree.map(lambda a: lax.all_gather(a, axis), part)

    def take(source):
        return jax.tree.map(lambda a: lax.dynamic_index_in_dim(a, source, 0, False), gathered)

    return lax.fori_loop(
        1, lax.axis_size(axis), lambda source, state: combine(state, take(source)), take(0)
    )


def block_partial(query_block, cache_keys, cache_values, valid_len, score_scale):
    scores = (
        lax.dot_general(
            query_block, cache_keys, (((1,), (1,)), ((), ())), preferred_element_type=jnp.float32
        )
        * score_scale
    )
    columns = jnp.arange(cache_keys.shape[0], dtype=jnp.int32)
    scores = jnp.where(columns[None, :] < valid_len, scores, -jnp.inf)
    row_max = jnp.max(scores, axis=1)
    weights = jnp.exp(scores - row_max[:, None])
    row_sum = jnp.sum(weights, axis=1)
    weighted = jnp.dot(
        weights.astype(jnp.bfloat16), cache_values, preferred_element_type=jnp.float32
    )
    return (row_max, row_sum, weighted)


def combine(first, second):
    top = jnp.maximum(first[0], second[0])
    left = jnp.exp(first[0] - top)
    right = jnp.exp(second[0] - top)
    return (
        top,
        left * first[1] + right * second[1],
        left[:, None] * first[2] + right[:, None] * second[2],
    )


def per_device(queries, cache_keys, cache_values, lengths, span_owner):
    device_index = lax.axis_index("seq")
    owner_index = span_owner[0]
    valid_len = lengths[device_index]
    head_size = cache_keys.shape[1]
    block = spread(queries, "seq", owner_index)
    span_len = queries.shape[1]
    total_rows = span_len * queries.shape[2] // head_size
    block_rows = min(512, total_rows)
    query_blocks = block.reshape(total_rows // block_rows, block_rows, head_size)
    score_scale = 1.0 / jnp.sqrt(jnp.float32(head_size))

    def one_block(query_block):
        return block_partial(query_block, cache_keys, cache_values, valid_len, score_scale)

    row_max, row_sum, weighted = lax.map(one_block, query_blocks)
    row_max = row_max.reshape(total_rows)
    row_sum = row_sum.reshape(total_rows)
    weighted = weighted.reshape(total_rows, head_size)
    top, denom, numer = combined_all((row_max, row_sum, weighted), "seq", combine)
    result = (numer / denom[:, None]).astype(jnp.bfloat16).reshape(1, span_len, queries.shape[2])
    return jnp.where(device_index == owner_index, result, jnp.zeros_like(result))


def solution(mesh):
    return jax.shard_map(
        per_device,
        mesh=mesh,
        in_specs=(P("seq", None, "head"), P("seq", "head"), P("seq", "head"), P(), P()),
        out_specs=P("seq", None, "head"),
        check_vma=False,
    )
```

profile of v0, /device:TPU:1, one launch (start us, length us, event | category | flops | bytes accessed | tf_op | source)
XLA Modules:
  0.0 445.9 jit_solution(10816783090056473754)
XLA Ops:
  7.2 1.0 reshape.28
  8.3 0.0 all-reduce.2.cloned.1.call-update
  8.3 0.0 all-gather.4.cloned.1.call-start
  8.4 1.3 dynamic_slice.48
  9.7 118.2 %all-reduce.2.cloned.1.call-done = bf16[4,512,128]{2,1,0:T(8,128)(2,1)} async-done(((bf16[4,512,128]{2,1,0:T(8,128)(2,1)}), bf16[4,512,128]{2,1,0:T(8,128)(2,1)}) %all-reduce.2.cloned.1.call-update) | async-done | bytes 524304 | tf_op jit(solution)/shard_map/psum | solution.py:9
  127.9 122.1 %while.33 = (s32[]{:T(128)}, f32[4,512]{1,0:T(4,128)S(1)}, f32[4,512]{1,0:T(4,128)S(1)}, f32[4,512,128]{2,1,0:T(8,128)}, s32[]{:T(128)}, /*index=5*/bf16[4,512,1...) while((s32[]{:T(128)}, f32[4,512]{1,0:T(4,128)S(1)}, ...), condition=%wide.region_4.5_spmd, body=%wide.region_1.4_spmd.sunk | while | flops 2193628160 | bytes 63357084 | solution.py:67
  127.9 0.7 iota_compare_fusion.2
  128.6 0.0 copy-start
  128.6 10.2 %fusion.32 = (f32[512]{0:T(512)S(1)}, f32[512,8192]{1,0:T(8,128)}) fusion(pred[8192]{0:T(1024)(128)(4,1)S(1)} %iota_compare_fusion.2, bf16[8192,128]{1,0:T(8,128)(2,1)} %get-tuple-element.403, bf16[4,512,128]{2,1,0:T(8,128)(2,1)} %get-tuple-element.402, s32[]{:T(128)S(6)} %copy.20), kind=kOutput, calls=%fused_computation.2.clone.1 | convolution fusion | flops 1086324224 | bytes 19015684 | tf_op jit(solution)/shard_map/while/body/eval_jaxpr/dot_general | solution.py:25
  138.8 9.8 %fusion.33 = f32[512]{0:T(512)S(1)} fusion(f32[512,8192]{1,0:T(8,128)} %get-tuple-element.363, f32[512]{0:T(512)S(1)} %get-tuple-element.362, pred[8192]{0:T(1024)(128)(4,1)S(1)} %iota_compare_fusion.2), kind=kLoop, calls=%fused_computation.4.clone.1 | loop fusion | flops 16776704 | bytes 16789504 | tf_op jit(solution)/shard_map/while/body/eval_jaxpr/reduce_sum | solution.py:34
  148.6 9.7 %fusion.34 = f32[4,512,128]{2,1,0:T(8,128)} fusion(f32[4,512,128]{2,1,0:T(8,128)} %get-tuple-element.390, s32[]{:T(128)S(6)} %copy.20, bf16[8192,128]{1,0:T(8,128)(2,1)S(1)} %copy-done, f32[512,8192]{1,0:T(8,128)} %get-tuple-element.363, f32[512]{0:T(512)S(1)} %get-tuple-element.362, pred[8192]{0:T(1024)(128)(4,1)S(1)} %iota_compare_fusion.2), kind=kOutput, calls=%fused_computation.8.clone.1 | convolution fusion | flops 1090519040 | bytes 19146756 | tf_op jit(solution)/shard_map/while/body/eval_jaxpr/dot_general | solution.py:35
  158.5 0.7 iota_compare_fusion.2
  159.2 10.2 %fusion.32 = (f32[512]{0:T(512)S(1)}, f32[512,8192]{1,0:T(8,128)}) fusion(pred[8192]{0:T(1024)(128)(4,1)S(1)} %iota_compare_fusion.2, bf16[8192,128]{1,0:T(8,128)(2,1)} %get-tuple-element.403, bf16[4,512,128]{2,1,0:T(8,128)(2,1)} %get-tuple-element.402, s32[]{:T(128)S(6)} %copy.20), kind=kOutput, calls=%fused_computation.2.clone.1 | convolution fusion | flops 1086324224 | bytes 19015684 | tf_op jit(solution)/shard_map/while/body/eval_jaxpr/dot_general | solution.py:25
  169.4 9.8 %fusion.33 = f32[512]{0:T(512)S(1)} fusion(f32[512,8192]{1,0:T(8,128)} %get-tuple-element.363, f32[512]{0:T(512)S(1)} %get-tuple-element.362, pred[8192]{0:T(1024)(128)(4,1)S(1)} %iota_compare_fusion.2), kind=kLoop, calls=%fused_computation.4.clone.1 | loop fusion | flops 16776704 | bytes 16789504 | tf_op jit(solution)/shard_map/while/body/eval_jaxpr/reduce_sum | solution.py:34
  179.2 9.7 %fusion.34 = f32[4,512,128]{2,1,0:T(8,128)} fusion(f32[4,512,128]{2,1,0:T(8,128)} %get-tuple-element.390, s32[]{:T(128)S(6)} %copy.20, bf16[8192,128]{1,0:T(8,128)(2,1)S(1)} %copy-done, f32[512,8192]{1,0:T(8,128)} %get-tuple-element.363, f32[512]{0:T(512)S(1)} %get-tuple-element.362, pred[8192]{0:T(1024)(128)(4,1)S(1)} %iota_compare_fusion.2), kind=kOutput, calls=%fused_computation.8.clone.1 | convolution fusion | flops 1090519040 | bytes 19146756 | tf_op jit(solution)/shard_map/while/body/eval_jaxpr/dot_general | solution.py:35
  189.0 0.7 iota_compare_fusion.2
  189.7 10.2 %fusion.32 = (f32[512]{0:T(512)S(1)}, f32[512,8192]{1,0:T(8,128)}) fusion(pred[8192]{0:T(1024)(128)(4,1)S(1)} %iota_compare_fusion.2, bf16[8192,128]{1,0:T(8,128)(2,1)} %get-tuple-element.403, bf16[4,512,128]{2,1,0:T(8,128)(2,1)} %get-tuple-element.402, s32[]{:T(128)S(6)} %copy.20), kind=kOutput, calls=%fused_computation.2.clone.1 | convolution fusion | flops 1086324224 | bytes 19015684 | tf_op jit(solution)/shard_map/while/body/eval_jaxpr/dot_general | solution.py:25
  199.9 9.8 %fusion.33 = f32[512]{0:T(512)S(1)} fusion(f32[512,8192]{1,0:T(8,128)} %get-tuple-element.363, f32[512]{0:T(512)S(1)} %get-tuple-element.362, pred[8192]{0:T(1024)(128)(4,1)S(1)} %iota_compare_fusion.2), kind=kLoop, calls=%fused_computation.4.clone.1 | loop fusion | flops 16776704 | bytes 16789504 | tf_op jit(solution)/shard_map/while/body/eval_jaxpr/reduce_sum | solution.py:34
  209.7 9.7 %fusion.34 = f32[4,512,128]{2,1,0:T(8,128)} fusion(f32[4,512,128]{2,1,0:T(8,128)} %get-tuple-element.390, s32[]{:T(128)S(6)} %copy.20, bf16[8192,128]{1,0:T(8,128)(2,1)S(1)} %copy-done, f32[512,8192]{1,0:T(8,128)} %get-tuple-element.363, f32[512]{0:T(512)S(1)} %get-tuple-element.362, pred[8192]{0:T(1024)(128)(4,1)S(1)} %iota_compare_fusion.2), kind=kOutput, calls=%fused_computation.8.clone.1 | convolution fusion | flops 1090519040 | bytes 19146756 | tf_op jit(solution)/shard_map/while/body/eval_jaxpr/dot_general | solution.py:35
  219.5 0.7 iota_compare_fusion.2
  220.2 10.2 %fusion.32 = (f32[512]{0:T(512)S(1)}, f32[512,8192]{1,0:T(8,128)}) fusion(pred[8192]{0:T(1024)(128)(4,1)S(1)} %iota_compare_fusion.2, bf16[8192,128]{1,0:T(8,128)(2,1)} %get-tuple-element.403, bf16[4,512,128]{2,1,0:T(8,128)(2,1)} %get-tuple-element.402, s32[]{:T(128)S(6)} %copy.20), kind=kOutput, calls=%fused_computation.2.clone.1 | convolution fusion | flops 1086324224 | bytes 19015684 | tf_op jit(solution)/shard_map/while/body/eval_jaxpr/dot_general | solution.py:25
  230.4 9.8 %fusion.33 = f32[512]{0:T(512)S(1)} fusion(f32[512,8192]{1,0:T(8,128)} %get-tuple-element.363, f32[512]{0:T(512)S(1)} %get-tuple-element.362, pred[8192]{0:T(1024)(128)(4,1)S(1)} %iota_compare_fusion.2), kind=kLoop, calls=%fused_computation.4.clone.1 | loop fusion | flops 16776704 | bytes 16789504 | tf_op jit(solution)/shard_map/while/body/eval_jaxpr/reduce_sum | solution.py:34
  240.2 9.7 %fusion.34 = f32[4,512,128]{2,1,0:T(8,128)} fusion(f32[4,512,128]{2,1,0:T(8,128)} %get-tuple-element.390, s32[]{:T(128)S(6)} %copy.20, bf16[8192,128]{1,0:T(8,128)(2,1)S(1)} %copy-done, f32[512,8192]{1,0:T(8,128)} %get-tuple-element.363, f32[512]{0:T(512)S(1)} %get-tuple-element.362, pred[8192]{0:T(1024)(128)(4,1)S(1)} %iota_compare_fusion.2), kind=kOutput, calls=%fused_computation.8.clone.1 | convolution fusion | flops 1090519040 | bytes 19146756 | tf_op jit(solution)/shard_map/while/body/eval_jaxpr/dot_general | solution.py:35
  250.1 0.0 all-gather.4.cloned.1.call-update
  250.1 26.0 %all-gather.1 = f32[32,1,2048]{2,1,0:T(1,128)S(1)} all-gather(f32[1,1,2048]{2,1,0:T(1,128)S(1)} %reshape.31), channel_id=1, replica_groups=mesh['seq'=32,'head'=8] {'seq'}, dimensions={0}, use_global_device_ids=true | all-gather | bytes 270336 | tf_op jit(solution)/shard_map/all_gather | solution.py:13
  276.1 0.1 copy.10
  276.2 22.1 %all-gather = f32[32,1,2048]{2,1,0:T(1,128)S(1)} all-gather(f32[1,1,2048]{2,1,0:T(1,128)S(1)} %reshape.29), channel_id=1, replica_groups=mesh['seq'=32,'head'=8] {'seq'}, dimensions={0}, use_global_device_ids=true | all-gather | bytes 270336 | tf_op jit(solution)/shard_map/all_gather | solution.py:13
  298.3 0.1 copy.11
  298.4 71.1 %all-gather.4.cloned.1.call-done = f32[32,2048,128]{2,1,0:T(8,128)} async-done(((f32[1,2048,128]{2,1,0:T(8,128)}), f32[32,2048,128]{2,1,0:T(8,128)}) %all-gather.4.cloned.1.call-update) | async-done | bytes 33554448 | tf_op jit(solution)/shard_map/all_gather | solution.py:13
  369.4 1.3 slice_bitcast_fusion
  370.7 67.0 %while.34 = (s32[]{:T(128)}, f32[2048]{0:T(1024)S(1)}, f32[2048]{0:T(1024)S(1)}, f32[2048,128]{1,0:T(8,128)S(1)}, f32[32,2048]{1,0:T(8,128)S(1)}, /*index=5*/f32...) while((s32[]{:T(128)}, f32[2048]{0:T(1024)S(1)}, f32[2048]{0:T(1024)S(1)}, ...), condition=%wide.region_6.7_spmd, body=%wide.region_5.6_spmd.sunk | while | flops 798725 | bytes 3260559 | solution.py:18
  370.8 2.1 fusion.35
  373.0 2.1 fusion.35
  375.1 2.1 fusion.35
  377.3 2.1 fusion.35
  379.5 2.1 fusion.35
  381.6 2.1 fusion.35
  383.8 2.1 fusion.35
  385.9 2.1 fusion.35
  388.1 2.1 fusion.35
  390.3 2.1 fusion.35
  392.4 2.1 fusion.35
  394.6 2.1 fusion.35
  396.7 2.1 fusion.35
  398.9 2.1 fusion.35
  401.1 2.1 fusion.35
  403.2 2.1 fusion.35
  405.4 2.1 fusion.35
  407.5 2.1 fusion.35
  409.7 2.1 fusion.35
  411.9 2.1 fusion.35
  414.0 2.1 fusion.35
  416.2 2.1 fusion.35
  418.3 2.1 fusion.35
  420.5 2.1 fusion.35
  422.7 2.1 fusion.35
  424.8 2.1 fusion.35
  427.0 2.1 fusion.35
  429.1 2.1 fusion.35
  431.3 2.1 fusion.35
  433.5 2.1 fusion.35
  435.6 2.1 fusion.35
  437.7 0.3 fusion.19
  438.1 1.0 select_n.54
  (86 shorter events, 1.5 us)
Async XLA Ops:
  6.5 121.4 %all-reduce.2.cloned.1.call-start = ((), (), s32[]{:S(2)}) async-start(), calls=%async_computation | async-start | bytes 1048576 | tf_op jit(solution)/shard_map/psum | solution.py:9
  8.3 361.1 %all-gather.4.cloned.1.call-start = ((), (), s32[]{:S(2)}) async-start(), calls=%async_computation.1 | async-start | bytes 34603008 | tf_op jit(solution)/shard_map/all_gather | solution.py:13
  128.6 20.0 %copy-start = (bf16[8192,128]{1,0:T(8,128)(2,1)S(1)}, bf16[8192,128]{1,0:T(8,128)(2,1)}, u32[]{:S(2)}) copy-start(bf16[8192,128]{1,0:T(8,128)(2,1)} %get-tuple-element.404) | copy-start | bytes 6291460 | tf_op jit(solution)/shard_map/while
  159.2 20.0 %copy-start = (bf16[8192,128]{1,0:T(8,128)(2,1)S(1)}, bf16[8192,128]{1,0:T(8,128)(2,1)}, u32[]{:S(2)}) copy-start(bf16[8192,128]{1,0:T(8,128)(2,1)} %get-tuple-element.404) | copy-start | bytes 6291460 | tf_op jit(solution)/shard_map/while
  189.7 20.0 %copy-start = (bf16[8192,128]{1,0:T(8,128)(2,1)S(1)}, bf16[8192,128]{1,0:T(8,128)(2,1)}, u32[]{:S(2)}) copy-start(bf16[8192,128]{1,0:T(8,128)(2,1)} %get-tuple-element.404) | copy-start | bytes 6291460 | tf_op jit(solution)/shard_map/while
  220.2 20.0 %copy-start = (bf16[8192,128]{1,0:T(8,128)(2,1)S(1)}, bf16[8192,128]{1,0:T(8,128)(2,1)}, u32[]{:S(2)}) copy-start(bf16[8192,128]{1,0:T(8,128)(2,1)} %get-tuple-element.404) | copy-start | bytes 6291460 | tf_op jit(solution)/shard_map/while
Sparse Core Ops, SparseCore 0:
  10.5 117.3 all-reduce.1
  250.2 119.2 all-gather.3
where the time goes:
time: 448 us; the launch traced here: 446 us
  waiting for transfers between devices  189 us (42%)
  other arithmetic  107 us (24%)
  matrix products  79.7 us (18%)
  blocking collectives  48.1 us (11%)
  between operations  14.1 us (3%)
  local copies, waits for them, and re-layouts  5.85 us (1%)
    psum x1, waiting for transfers between devices, spread(): return lax.psum(jnp.where(mine, array, jnp.zeros_like(array)), axis)  118 us
    all_gather x1, waiting for transfers between devices, combined_all(): gathered = jax.tree.map(lambda a: lax.all_gather(a, axis), part)  71.1 us
    add x31, other arithmetic, combine(): left[:, None] * first[2] + right[:, None] * second[2]  64.7 us
    all_gather x2, blocking collectives, combined_all(): gathered = jax.tree.map(lambda a: lax.all_gather(a, axis), part)  48.1 us
    dot_general x4, matrix products, block_partial(): lax.dot_general(query_block, cache_keys, (((1,), (1,)), ((), ())), prefer...  40.8 us
    reduce_sum x4, other arithmetic, block_partial(): row_sum = jnp.sum(weights, axis=1)  39.2 us
    dot_general x4, matrix products, block_partial(): jnp.dot(weights.astype(jnp.bfloat16), cache_values, preferred_element_typ...  38.9 us
  transfers between devices with their start and end apart: 2, of which 2 were waited for; matrix products, arithmetic and copies ran while one was open for 0% of the time, Pallas kernels for 0%

commit v1 on v0

--- a/solution.py
+++ b/solution.py
@@ -3,10 +3,12 @@
 from jax import lax
 from jax.sharding import PartitionSpec as P
 
+strings_process = lambda body, named_axis: lax.all_gather(body, axis_name=named_axis).sum(axis=0)
+
 
 def spread(array, axis, root):
     mine = lax.axis_index(axis) == root
-    return lax.psum(jnp.where(mine, array, jnp.zeros_like(array)), axis)
+    return strings_process(jnp.where(mine, array, jnp.zeros_like(array)), axis)
 
 
 def combined_all(part, axis, combine):

time: 448 us -> 410 us (0.915)
  waiting for transfers between devices: 189 us -> 154 us
  matrix products: 79.7 us -> 69.5 us
  other arithmetic: 107 us -> 117 us
    psum x1 -> x0, waiting for transfers between devices: 118 us -> none  [spread(): return lax.psum(jnp.where(mine, array, jnp.zeros_like(array)), axis)]
    all_gather x0 -> x1, waiting for transfers between devices: none -> 82.1 us  [lax.all_gather(body, axis_name=named_axis).sum(axis=0)]
    dot_general x4, matrix products: 40.8 us -> 28.2 us  [block_partial(): lax.dot_general(query_block, cache_keys, (((1,), (1,)), ((), ())), prefer...]
    reduce_sum x0 -> x1, other arithmetic: none -> 8.86 us  [lax.all_gather(body, axis_name=named_axis).sum(axis=0)]
where the time goes in v1:
time: 410 us; the launch traced here: 408 us
  waiting for transfers between devices  154 us (38%)
  other arithmetic  117 us (29%)
  matrix products  69.5 us (17%)
  blocking collectives  47.3 us (12%)
  between operations  14.3 us (3%)
  local copies, waits for them, and re-layouts  4.98 us (1%)
    all_gather x1, waiting for transfers between devices, lax.all_gather(body, axis_name=named_axis).sum(axis=0)  82.1 us
    all_gather x1, waiting for transfers between devices, combined_all(): gathered = jax.tree.map(lambda a: lax.all_gather(a, axis), part)  71.4 us
    add x31, other arithmetic, combine(): left[:, None] * first[2] + right[:, None] * second[2]  64.7 us
    all_gather x2, blocking collectives, combined_all(): gathered = jax.tree.map(lambda a: lax.all_gather(a, axis), part)  47.3 us
    dot_general x4, matrix products, block_partial(): jnp.dot(weights.astype(jnp.bfloat16), cache_values, preferred_element_typ...  41.3 us
    reduce_sum x4, other arithmetic, block_partial(): row_sum = jnp.sum(weights, axis=1)  39.2 us
    dot_general x4, matrix products, block_partial(): lax.dot_general(query_block, cache_keys, (((1,), (1,)), ((), ())), prefer...  28.2 us
    reduce_sum x1, other arithmetic, lax.all_gather(body, axis_name=named_axis).sum(axis=0)  8.86 us
  transfers between devices with their start and end apart: 2, of which 2 were waited for; matrix products, arithmetic and copies ran while one was open for 0% of the time, Pallas kernels for 0%

profile of v1, /device:TPU:1, one launch (start us, length us, event | category | flops | bytes accessed | tf_op | source)
XLA Modules:
  0.0 407.9 jit_solution(12268753457291387873)
XLA Ops:
  7.3 0.8 broadcast_select_fusion
  8.2 0.0 all-gather.6.cloned.1.call-start
  8.3 1.3 dynamic_slice.48
  9.5 82.1 %all-gather.8.cloned.1.call-done = bf16[32,128,2048]{2,1,0:T(8,128)(2,1)} async-done(((bf16[1,128,2048]{2,1,0:T(8,128)(2,1)}), bf16[32,128,2048]{2,1,0:T(8,128)(2,1)}) %all-gather.8.cloned.1.call-update) | async-done | bytes 16777232 | tf_op jit(solution)/shard_map/all_gather | solution.py:6
  91.7 8.9 %reduce.2 = bf16[128,2048]{1,0:T(8,128)(2,1)S(1)} reduce(bf16[32,128,2048]{2,1,0:T(8,128)(2,1)} %all-gather.8.cloned.1.call-done, bf16[]{:T(256)} %constant.84.clone.1), dimensions={0}, to_apply=%region_0.1 | reduce | flops 8126464 | bytes 17301506 | tf_op jit(solution)/shard_map/reduce_sum | solution.py:6
  100.5 0.2 reshape.30
  100.8 111.7 %while.33 = (s32[]{:T(128)}, f32[4,512]{1,0:T(4,128)S(1)}, f32[4,512]{1,0:T(4,128)S(1)}, f32[4,512,128]{2,1,0:T(8,128)}, s32[]{:T(128)}, /*index=5*/bf16[4,512,1...) while((s32[]{:T(128)}, f32[4,512]{1,0:T(4,128)S(1)}, ...), condition=%wide.region_4.5_spmd, body=%wide.region_1.4_spmd.sunk | while | flops 2193628160 | bytes 54968448 | solution.py:69
  100.8 0.6 iota_compare_fusion.2
  101.4 7.1 %fusion.32 = (f32[512]{0:T(512)S(1)}, f32[512,8192]{1,0:T(8,128)}) fusion(pred[8192]{0:T(1024)(128)(4,1)S(1)} %iota_compare_fusion.2, bf16[8192,128]{1,0:T(8,128)(2,1)S(1)} %get-tuple-element.403, bf16[4,512,128]{2,1,0:T(8,128)(2,1)S(1)} %get-tuple-element.402, s32[]{:T(128)S(6)} %copy.19), kind=kOutput, calls=%fused_computation.2.clone.1 | convolution fusion | flops 1086324224 | bytes 19015684 | tf_op jit(solution)/shard_map/while/body/eval_jaxpr/dot_general | solution.py:27
  108.5 9.8 %fusion.33 = f32[512]{0:T(512)S(1)} fusion(f32[512,8192]{1,0:T(8,128)} %get-tuple-element.363, f32[512]{0:T(512)S(1)} %get-tuple-element.362, pred[8192]{0:T(1024)(128)(4,1)S(1)} %iota_compare_fusion.2), kind=kLoop, calls=%fused_computation.4.clone.1 | loop fusion | flops 16776704 | bytes 16789504 | tf_op jit(solution)/shard_map/while/body/eval_jaxpr/reduce_sum | solution.py:36
  118.3 10.3 %fusion.34 = f32[4,512,128]{2,1,0:T(8,128)} fusion(f32[4,512,128]{2,1,0:T(8,128)} %get-tuple-element.390, s32[]{:T(128)S(6)} %copy.19, bf16[8192,128]{1,0:T(8,128)(2,1)} %get-tuple-element.404, f32[512,8192]{1,0:T(8,128)} %get-tuple-element.363, f32[512]{0:T(512)S(1)} %get-tuple-element.362, pred[8192]{0:T(1024)(128)(4,1)S(1)} %iota_compare_fusion.2), kind=kOutput, calls=%fused_computation.8.clone.1 | convolution fusion | flops 1090519040 | bytes 19146756 | tf_op jit(solution)/shard_map/while/body/eval_jaxpr/dot_general | solution.py:37
  128.7 0.6 iota_compare_fusion.2
  129.4 7.1 %fusion.32 = (f32[512]{0:T(512)S(1)}, f32[512,8192]{1,0:T(8,128)}) fusion(pred[8192]{0:T(1024)(128)(4,1)S(1)} %iota_compare_fusion.2, bf16[8192,128]{1,0:T(8,128)(2,1)S(1)} %get-tuple-element.403, bf16[4,512,128]{2,1,0:T(8,128)(2,1)S(1)} %get-tuple-element.402, s32[]{:T(128)S(6)} %copy.19), kind=kOutput, calls=%fused_computation.2.clone.1 | convolution fusion | flops 1086324224 | bytes 19015684 | tf_op jit(solution)/shard_map/while/body/eval_jaxpr/dot_general | solution.py:27
  136.4 9.8 %fusion.33 = f32[512]{0:T(512)S(1)} fusion(f32[512,8192]{1,0:T(8,128)} %get-tuple-element.363, f32[512]{0:T(512)S(1)} %get-tuple-element.362, pred[8192]{0:T(1024)(128)(4,1)S(1)} %iota_compare_fusion.2), kind=kLoop, calls=%fused_computation.4.clone.1 | loop fusion | flops 16776704 | bytes 16789504 | tf_op jit(solution)/shard_map/while/body/eval_jaxpr/reduce_sum | solution.py:36
  146.2 10.3 %fusion.34 = f32[4,512,128]{2,1,0:T(8,128)} fusion(f32[4,512,128]{2,1,0:T(8,128)} %get-tuple-element.390, s32[]{:T(128)S(6)} %copy.19, bf16[8192,128]{1,0:T(8,128)(2,1)} %get-tuple-element.404, f32[512,8192]{1,0:T(8,128)} %get-tuple-element.363, f32[512]{0:T(512)S(1)} %get-tuple-element.362, pred[8192]{0:T(1024)(128)(4,1)S(1)} %iota_compare_fusion.2), kind=kOutput, calls=%fused_computation.8.clone.1 | convolution fusion | flops 1090519040 | bytes 19146756 | tf_op jit(solution)/shard_map/while/body/eval_jaxpr/dot_general | solution.py:37
  156.6 0.6 iota_compare_fusion.2
  157.3 7.1 %fusion.32 = (f32[512]{0:T(512)S(1)}, f32[512,8192]{1,0:T(8,128)}) fusion(pred[8192]{0:T(1024)(128)(4,1)S(1)} %iota_compare_fusion.2, bf16[8192,128]{1,0:T(8,128)(2,1)S(1)} %get-tuple-element.403, bf16[4,512,128]{2,1,0:T(8,128)(2,1)S(1)} %get-tuple-element.402, s32[]{:T(128)S(6)} %copy.19), kind=kOutput, calls=%fused_computation.2.clone.1 | convolution fusion | flops 1086324224 | bytes 19015684 | tf_op jit(solution)/shard_map/while/body/eval_jaxpr/dot_general | solution.py:27
  164.3 9.8 %fusion.33 = f32[512]{0:T(512)S(1)} fusion(f32[512,8192]{1,0:T(8,128)} %get-tuple-element.363, f32[512]{0:T(512)S(1)} %get-tuple-element.362, pred[8192]{0:T(1024)(128)(4,1)S(1)} %iota_compare_fusion.2), kind=kLoop, calls=%fused_computation.4.clone.1 | loop fusion | flops 16776704 | bytes 16789504 | tf_op jit(solution)/shard_map/while/body/eval_jaxpr/reduce_sum | solution.py:36
  174.1 10.3 %fusion.34 = f32[4,512,128]{2,1,0:T(8,128)} fusion(f32[4,512,128]{2,1,0:T(8,128)} %get-tuple-element.390, s32[]{:T(128)S(6)} %copy.19, bf16[8192,128]{1,0:T(8,128)(2,1)} %get-tuple-element.404, f32[512,8192]{1,0:T(8,128)} %get-tuple-element.363, f32[512]{0:T(512)S(1)} %get-tuple-element.362, pred[8192]{0:T(1024)(128)(4,1)S(1)} %iota_compare_fusion.2), kind=kOutput, calls=%fused_computation.8.clone.1 | convolution fusion | flops 1090519040 | bytes 19146756 | tf_op jit(solution)/shard_map/while/body/eval_jaxpr/dot_general | solution.py:37
  184.6 0.6 iota_compare_fusion.2
  185.2 7.1 %fusion.32 = (f32[512]{0:T(512)S(1)}, f32[512,8192]{1,0:T(8,128)}) fusion(pred[8192]{0:T(1024)(128)(4,1)S(1)} %iota_compare_fusion.2, bf16[8192,128]{1,0:T(8,128)(2,1)S(1)} %get-tuple-element.403, bf16[4,512,128]{2,1,0:T(8,128)(2,1)S(1)} %get-tuple-element.402, s32[]{:T(128)S(6)} %copy.19), kind=kOutput, calls=%fused_computation.2.clone.1 | convolution fusion | flops 1086324224 | bytes 19015684 | tf_op jit(solution)/shard_map/while/body/eval_jaxpr/dot_general | solution.py:27
  192.3 9.8 %fusion.33 = f32[512]{0:T(512)S(1)} fusion(f32[512,8192]{1,0:T(8,128)} %get-tuple-element.363, f32[512]{0:T(512)S(1)} %get-tuple-element.362, pred[8192]{0:T(1024)(128)(4,1)S(1)} %iota_compare_fusion.2), kind=kLoop, calls=%fused_computation.4.clone.1 | loop fusion | flops 16776704 | bytes 16789504 | tf_op jit(solution)/shard_map/while/body/eval_jaxpr/reduce_sum | solution.py:36
  202.0 10.3 %fusion.34 = f32[4,512,128]{2,1,0:T(8,128)} fusion(f32[4,512,128]{2,1,0:T(8,128)} %get-tuple-element.390, s32[]{:T(128)S(6)} %copy.19, bf16[8192,128]{1,0:T(8,128)(2,1)} %get-tuple-element.404, f32[512,8192]{1,0:T(8,128)} %get-tuple-element.363, f32[512]{0:T(512)S(1)} %get-tuple-element.362, pred[8192]{0:T(1024)(128)(4,1)S(1)} %iota_compare_fusion.2), kind=kOutput, calls=%fused_computation.8.clone.1 | convolution fusion | flops 1090519040 | bytes 19146756 | tf_op jit(solution)/shard_map/while/body/eval_jaxpr/dot_general | solution.py:37
  212.5 0.0 all-gather.6.cloned.1.call-update
  212.5 24.5 %all-gather.2 = f32[32,1,2048]{2,1,0:T(1,128)S(1)} all-gather(f32[1,1,2048]{2,1,0:T(1,128)S(1)} %reshape.35), channel_id=1, replica_groups=mesh['seq'=32,'head'=8] {'seq'}, dimensions={0}, use_global_device_ids=true | all-gather | bytes 270336 | tf_op jit(solution)/shard_map/all_gather | solution.py:15
  237.0 0.1 copy.10
  237.1 22.8 %all-gather.1 = f32[32,1,2048]{2,1,0:T(1,128)S(1)} all-gather(f32[1,1,2048]{2,1,0:T(1,128)S(1)} %reshape.33), channel_id=1, replica_groups=mesh['seq'=32,'head'=8] {'seq'}, dimensions={0}, use_global_device_ids=true | all-gather | bytes 270336 | tf_op jit(solution)/shard_map/all_gather | solution.py:15
  259.9 0.1 copy.11
  260.0 71.4 %all-gather.6.cloned.1.call-done = f32[32,2048,128]{2,1,0:T(8,128)} async-done(((f32[1,2048,128]{2,1,0:T(8,128)}), f32[32,2048,128]{2,1,0:T(8,128)}) %all-gather.6.cloned.1.call-update) | async-done | bytes 33554448 | tf_op jit(solution)/shard_map/all_gather | solution.py:15
  331.4 1.3 slice_bitcast_fusion
  332.7 67.0 %while.34 = (s32[]{:T(128)}, f32[2048]{0:T(1024)S(1)}, f32[2048]{0:T(1024)S(1)}, f32[2048,128]{1,0:T(8,128)S(1)}, f32[32,2048]{1,0:T(8,128)S(1)}, /*index=5*/f32...) while((s32[]{:T(128)}, f32[2048]{0:T(1024)S(1)}, f32[2048]{0:T(1024)S(1)}, ...), condition=%wide.region_6.7_spmd, body=%wide.region_5.6_spmd.sunk | while | flops 798725 | bytes 3260559 | solution.py:20
  332.8 2.1 fusion.35
  334.9 2.1 fusion.35
  337.1 2.1 fusion.35
  339.2 2.1 fusion.35
  341.4 2.1 fusion.35
  343.6 2.1 fusion.35
  345.7 2.1 fusion.35
  347.9 2.1 fusion.35
  350.0 2.1 fusion.35
  352.2 2.1 fusion.35
  354.4 2.1 fusion.35
  356.5 2.1 fusion.35
  358.7 2.1 fusion.35
  360.8 2.1 fusion.35
  363.0 2.1 fusion.35
  365.2 2.1 fusion.35
  367.3 2.1 fusion.35
  369.5 2.1 fusion.35
  371.6 2.1 fusion.35
  373.8 2.1 fusion.35
  376.0 2.1 fusion.35
  378.1 2.1 fusion.35
  380.3 2.1 fusion.35
  382.4 2.1 fusion.35
  384.6 2.1 fusion.35
  386.8 2.1 fusion.35
  388.9 2.1 fusion.35
  391.1 2.1 fusion.35
  393.2 2.1 fusion.35
  395.4 2.1 fusion.35
  397.6 2.1 fusion.35
  399.7 0.3 fusion.19
  400.0 1.0 select_n.54
  (81 shorter events, 1.5 us)
Async XLA Ops:
  6.5 94.3 %copy-start = (bf16[8192,128]{1,0:T(8,128)(2,1)S(1)}, bf16[8192,128]{1,0:T(8,128)(2,1)}, u32[]{:S(2)}) copy-start(bf16[8192,128]{1,0:T(8,128)(2,1)} %param.10) | copy-start | bytes 6291460
  6.5 85.1 %all-gather.8.cloned.1.call-start = ((), (), s32[]{:S(2)}) async-start(), calls=%async_computation.1 | async-start | bytes 17301504 | tf_op jit(solution)/shard_map/all_gather | solution.py:6
  8.2 323.2 %all-gather.6.cloned.1.call-start = ((), (), s32[]{:S(2)}) async-start(), calls=%async_computation | async-start | bytes 34603008 | tf_op jit(solution)/shard_map/all_gather | solution.py:15
Sparse Core Ops, SparseCore 0:
  9.9 81.7 all-gather.7
  212.6 118.7 all-gather.5
